TPU v7x, 256 devices: a whole 4x4x8 slice. The times are simulated.
256 devices in a mesh: ri: 8 (over y, core), mu: 4 (over x), nu: 8 (over z).
Axes of the slice: x: 4, y: 4, z: 8, core: 2. Of those that a mesh axis runs over, the one named last changes fastest.
Arguments:
- three_center: bfloat16 [32, 2304, 128, 128], P('ri', ('mu', 'nu')), may hold values from -0.15625 to 0.15625
- block_pairs: int32 [2304, 2], P(('mu', 'nu')), may hold values from -1 to 95, as said below
- occ_factor: bfloat16 [12288, 128], P(('mu', 'nu')), may hold values from -6 to 6
- virt_density: bfloat16 [12288, 12288], P(('mu', 'nu'), 'ri'), may hold values from -0.0546875 to 0.0546875
- block_sizes: int32 [96], replicated, may hold values from 96 to 128
- occ_mask: int32 [96], replicated, may hold values 0 or 1
- virt_mask: int32 [96, 96], replicated, may hold values 0 or 1
Outputs:
- transformed: bfloat16 [32, 12288, 128], P('ri', ('mu', 'nu'))
Inputs may be any that keep to these rules, and one draw needn't show every extreme that they name: `block_pairs`: slots k in [d * 72, (d + 1) * 72) belong to device d of mu+nu; a live slot holds a mu block of that device's mu range (the range of 24 blocks of its mu index) and any nu block; empty slots hold -1 in both columns, and the live slots of a device come first. Every mu block appears in exactly 12 live slots, with distinct nu blocks. A device holds at most 72 live slots, and in every mu range some device holds exactly 72.
All inputs are finite; a program needn't handle non-finite values.
Results may differ from a plain program's by a relative error of at most 0.015.
Values may be sent and summed in bfloat16 or wider, within the bound.
A program may use at most 128 MiB of HBM per device.

v0:
```python
import jax
import jax.numpy as jnp
from jax import lax
from jax.sharding import PartitionSpec as P

BS = 128
NB = 96


def body(three_center, block_pairs, occ_factor, virt_density, block_sizes, occ_mask, virt_mask):
    rows_dev = virt_density.shape[0]
    occ_cols = occ_factor.shape[1]
    ri_rows = three_center.shape[0]
    blocks_mu = NB // lax.axis_size("mu")
    total_rows = NB * BS
    inside = jnp.arange(BS, dtype=jnp.int32)[None, :] < block_sizes[:, None]
    keep_occ = (inside & (occ_mask[:, None] > 0)).reshape(total_rows)
    gathered_occ = lax.all_gather(occ_factor, ("mu", "nu"), axis=0, tiled=True)
    occ_kept = jnp.where(keep_occ[:, None], gathered_occ, jnp.zeros((), jnp.bfloat16))
    mu_block = block_pairs[:, 0]
    nu_block = jnp.clip(block_pairs[:, 1], 0, NB - 1)
    slot_live = mu_block >= 0
    occ_blocks = occ_kept.reshape(NB, BS, occ_cols)[nu_block]
    products = jnp.einsum(
        "pkab,kbo->pkao", three_center, occ_blocks, preferred_element_type=jnp.float32
    )
    local_block = mu_block - lax.axis_index("mu") * blocks_mu
    segment_ids = jnp.where(slot_live, local_block, blocks_mu)

    def slot_sum(slab_products):
        return jax.ops.segment_sum(slab_products, segment_ids, num_segments=blocks_mu + 1)[
            :blocks_mu
        ]

    partial_value = jax.vmap(slot_sum)(products)
    partial_value = partial_value.reshape(ri_rows, blocks_mu * BS, occ_cols)
    virt_all = lax.all_gather(virt_density, "ri", axis=1, tiled=True)
    row_start = (lax.axis_index("mu") * lax.axis_size("nu") + lax.axis_index("nu")) * rows_dev
    row_ids = row_start + jnp.arange(rows_dev, dtype=jnp.int32)
    block_pick = (row_ids[:, None] // BS == jnp.arange(NB, dtype=jnp.int32)[None, :]).astype(
        jnp.float32
    )
    mask_rows = jnp.dot(block_pick, virt_mask.astype(jnp.float32)) > 0.5
    row_inside = lax.dynamic_slice_in_dim(inside.reshape(total_rows), row_start, rows_dev)
    keep_virt = (mask_rows[:, :, None] & inside[None, :, :] & row_inside[:, None, None]).reshape(
        rows_dev, total_rows
    )
    virt_kept = jnp.where(keep_virt, virt_all, jnp.zeros((), jnp.bfloat16))
    summed = lax.psum_scatter(
        partial_value.astype(jnp.bfloat16), "nu", scatter_dimension=1, tiled=True
    )
    result = jnp.einsum(
        "sm,pmo->pso",
        virt_kept,
        lax.all_gather(summed, ("mu", "nu"), axis=1, tiled=True),
        preferred_element_type=jnp.float32,
    )
    return result.astype(jnp.bfloat16)


def solution(mesh):
    in_specs = (
        P("ri", ("mu", "nu"), None, None),
        P(("mu", "nu"), None),
        P(("mu", "nu"), None),
        P(("mu", "nu"), "ri"),
        P(),
        P(),
        P(),
    )
    out_specs = P("ri", ("mu", "nu"), None)
    return jax.shard_map(body, mesh=mesh, in_specs=in_specs, out_specs=out_specs, check_vma=False)
```

profile of v0, /device:TPU:8, one launch (start us, length us, event | category | flops | bytes accessed | tf_op | source)
XLA Modules:
  0.0 418.7 jit_solution(11618415687132992076)
XLA Ops:
  7.4 0.7 all-gather.4.cloned.1.call-update
  8.1 0.8 fusion.26
  8.9 0.7 broadcast_compare_fusion
  9.6 0.7 bitcast_compare_fusion
  10.3 83.2 %all-gather.4.cloned.1.call-done = bf16[12288,128]{1,0:T(8,128)(2,1)} async-done(((bf16[384,128]{1,0:T(8,128)(2,1)}), bf16[12288,128]{1,0:T(8,128)(2,1)}) %all-gather.4.cloned.1.call-update) | async-done | bytes 3145744 | tf_op jit(solution)/shard_map/all_gather | solution.py:18
  93.5 8.4 %broadcast_select_fusion = bf16[12288,128]{1,0:T(8,128)(2,1)S(1)} fusion(bf16[12288,128]{1,0:T(8,128)(2,1)} %all-gather.4.cloned.1.call-done, pred[12288]{0:T(1024)(128)(4,1)S(1)} %get-tuple-element.8), kind=kLoop, calls=%fused_computation.15 | loop fusion | flops 1572864 | bytes 6303744 | tf_op jit(solution)/shard_map/jit(_where)/select_n | solution.py:19
  102.0 2.4 gather_fusion
  104.4 13.5 %fusion.9 = f32[72,4,128,128]{2,3,1,0:T(8,128)} fusion(bf16[4,72,128,128]{3,2,1,0:T(8,128)(2,1)} %param.7, bf16[72,128,128]{2,1,0:T(8,128)(2,1)} %gather_fusion), kind=kOutput, calls=%fused_computation.11 | convolution fusion | flops 1207959552 | bytes 30670848 | tf_op jit(solution)/shard_map/pkab,kbo->pkao/dot_general | solution.py:24
  117.9 18.6 %copy.19 = f32[72,4,128,128]{3,2,1,0:T(8,128)} copy(f32[72,4,128,128]{2,3,1,0:T(8,128)} %fusion.9) | data formatting | bytes 37748736 | tf_op jit(solution)/shard_map/pkab,kbo->pkao/transpose | solution.py:24
  136.5 3.5 broadcast_in_dim.21
  140.1 41.2 %scatter_fusion = f32[4,25,128,128]{3,2,1,0:T(8,128)} fusion(f32[4,25,128,128]{3,2,1,0:T(8,128)} %broadcast_in_dim.21, s32[72]{0:T(128)S(1)} %get-tuple-element.6, f32[72,4,128,128]{3,2,1,0:T(8,128)} %copy.19), kind=kCustom, calls=%fused_computation.1 | custom fusion | flops 4718592 | bytes 56623392 | tf_op jit(solution)/shard_map/vmap()/scatter-add | solution.py:31
  181.3 3.5 slice.19
  184.8 15.0 %copy.26 = bf16[4,3072,128]{2,0,1:T(4,128)(2,1)S(1)} copy(bf16[4,3072,128]{2,1,0:T(8,128)(2,1)S(1)} %bitcast.57) | data formatting | bytes 6291456
  199.8 2.2 copy.44
  202.1 0.5 all-gather.8.cloned.1.call-update
  202.9 43.4 %reduce-scatter.4.cloned.1.call-done = bf16[384,512]{1,0:T(8,128)(2,1)} async-done(((bf16[3072,512]{1,0:T(8,128)(2,1)}), bf16[384,512]{1,0:T(8,128)(2,1)}) %reduce-scatter.4.cloned.1.call-update) | async-done | bytes 393232
  246.2 1.1 reshape.109
  247.3 1.0 copy.27
  248.4 0.3 convolution_compare_fusion
  249.1 8.2 %all-gather.8.cloned.1.call-done = bf16[384,12288]{1,0:T(8,128)(2,1)} async-done(((bf16[384,1536]{1,0:T(8,128)(2,1)}), bf16[384,12288]{1,0:T(8,128)(2,1)}) %all-gather.8.cloned.1.call-update) | async-done | bytes 9437200 | tf_op jit(solution)/shard_map/all_gather | solution.py:37
  257.3 129.7 %all-gather.6.cloned.1.call-done = bf16[4,12288,128]{1,2,0:T(8,128)(2,1)} async-done(((bf16[4,384,128]{1,2,0:T(8,128)(2,1)}), bf16[4,12288,128]{1,2,0:T(8,128)(2,1)}) %all-gather.6.cloned.1.call-update) | async-done | bytes 12582928 | tf_op jit(solution)/shard_map/all_gather | solution.py:55
  386.9 6.7 %and.60 = pred[384,96,128]{2,1,0:T(32,128)(4,1)S(1)} broadcast(pred[384,96]{1,0:T(8,128)(4,1)S(1)} %copy.21), dimensions={0,1} | broadcast | bytes 4755456 | tf_op jit(solution)/shard_map/and | solution.py:45
  393.6 16.7 %fusion.17 = bf16[4,384,128]{1,2,0:T(8,128)(2,1)S(1)} fusion(bf16[4,12288,128]{1,2,0:T(8,128)(2,1)} %all-gather.6.cloned.1.call-done, bf16[384,12288]{1,0:T(8,128)(2,1)} %all-gather.8.cloned.1.call-done, pred[48,8,96,128]{3,2,1,0:T(32,128)(4,1)S(1)} %bitcast.60, pred[384]{0:T(512)(128)(4,1)S(1)} %dynamic_slice.3, pred[12288]{0:T(1024)(128)(4,1)S(1)} %bitcast_compare_fusion.1), kind=kOutput, calls=%fused_computation.18 | convolution fusion | flops 4846190592 | bytes 27144576 | tf_op jit(solution)/shard_map/sm,pmo->pso/dot_general | solution.py:52
  410.3 0.9 copy.22
  (16 shorter events, 0.8 us)
Async XLA Ops:
  7.4 86.1 %all-gather.4.cloned.1.call-start = ((), (), s32[]{:S(2)}) async-start(), calls=%async_computation.1 | async-start | bytes 3244032 | tf_op jit(solution)/shard_map/all_gather | solution.py:18
  8.1 238.1 %reduce-scatter.4.cloned.1.call-start = ((), (), s32[]{:S(2)}) async-start(), calls=%async_computation.4 | async-start | bytes 3538944
  202.0 46.3 %copy-start.1 = (s32[96,96]{1,0:T(8,128)S(1)}, s32[96,96]{1,0:T(8,128)}, u32[]{:S(2)}) copy-start(s32[96,96]{1,0:T(8,128)} %param.13) | copy-start | bytes 110596
  202.0 46.9 %copy-start = (s32[96]{0:T(128)S(1)}, s32[96]{0:T(128)}, u32[]{:S(2)}) copy-start(s32[96]{0:T(128)} %param.11) | copy-start | bytes 1156
  202.0 55.2 %all-gather.8.cloned.1.call-start = ((), (), s32[]{:S(2)}) async-start(), calls=%async_computation.3 | async-start | bytes 10616832 | tf_op jit(solution)/shard_map/all_gather | solution.py:37
  202.6 184.3 %all-gather.6.cloned.1.call-start = ((), (), s32[]{:S(2)}) async-start(), calls=%async_computation.2 | async-start | bytes 12976128 | tf_op jit(solution)/shard_map/all_gather | solution.py:55
Sparse Core Ops, SparseCore 0:
  10.8 82.6 all-gather.3
  202.2 43.9 reduce-scatter.3
Sparse Core Ops, SparseCore 1:
  204.4 52.9 all-gather.7
  259.6 127.2 all-gather.5
where the time goes:
time: 419 us
  waiting for transfers between devices  266 us (63%)
  local copies, waits for them, and re-layouts  55.4 us (13%)
  other arithmetic  51.9 us (12%)
  matrix products  30.5 us (7%)
  between operations  15 us (4%)
    all_gather x1, waiting for transfers between devices, body(): lax.all_gather(summed, ('mu', 'nu'), axis=1, tiled=True)  130 us
    all_gather x1, waiting for transfers between devices, body(): gathered_occ = lax.all_gather(occ_factor, ('mu', 'nu'), axis=0, tiled=True)  83.2 us
    unnamed x5, waiting for transfers between devices  44.6 us
    scatter-add x1, other arithmetic, slot_sum(): jax.ops.segment_sum(slab_products, segment_ids, num_segments=blocks_mu + 1)  41.2 us
    unnamed x8, local copies, waits for them, and re-layouts  19.3 us
    transpose x1, local copies, waits for them, and re-layouts, body(): jnp.einsum('pkab,kbo->pkao', three_center, occ_blocks, preferred_element_...  18.6 us
    dot_general x1, matrix products, body(): jnp.einsum('sm,pmo->pso', virt_kept, lax.all_gather(summed, ('mu', 'nu'),...  16.7 us
    dot_general x1, matrix products, body(): jnp.einsum('pkab,kbo->pkao', three_center, occ_blocks, preferred_element_...  13.5 us
  transfers between devices with their start and end apart: 4, of which 4 were waited for; matrix products, arithmetic and copies ran while one was open for 1% of the time, Pallas kernels for 0%

commit v1 on v0

--- a/solution.py
+++ b/solution.py
@@ -5,6 +5,21 @@
 
 BS = 128
 NB = 96
+
+
+def form_the_sums_all(vec):
+    degree = lax.psum(1, "ri")
+    m_next = sorted(((w, (w + 1) % degree) for w in range(degree)))
+    moved = vec
+    h = 1
+    cards = [moved]
+    while h < degree:
+        moved = lax.ppermute(moved, axis_name="ri", perm=m_next)
+        cards.insert(0, moved)
+        h = h + 1
+    found_now = jnp.concatenate(cards, axis=1)
+    val2 = lax.axis_index("ri") + 1
+    return jnp.roll(found_now, val2 * vec.shape[1], 1)
 
 
 def body(three_center, block_pairs, occ_factor, virt_density, block_sizes, occ_mask, virt_mask):
@@ -34,7 +49,7 @@
 
     partial_value = jax.vmap(slot_sum)(products)
     partial_value = partial_value.reshape(ri_rows, blocks_mu * BS, occ_cols)
-    virt_all = lax.all_gather(virt_density, "ri", axis=1, tiled=True)
+    virt_all = form_the_sums_all(virt_density)
     row_start = (lax.axis_index("mu") * lax.axis_size("nu") + lax.axis_index("nu")) * rows_dev
     row_ids = row_start + jnp.arange(rows_dev, dtype=jnp.int32)
     block_pick = (row_ids[:, None] // BS == jnp.arange(NB, dtype=jnp.int32)[None, :]).astype(

time: 419 us -> 429 us (1.024)
  the two profiles are of different devices: /device:TPU:8 before, /device:TPU:2 now
where the time goes in v1:
time: 429 us; the launch traced here: 428 us
  waiting for transfers between devices  242 us (56%)
  local copies, waits for them, and re-layouts  87.5 us (20%)
  other arithmetic  51.3 us (12%)
  matrix products  33.6 us (8%)
  between operations  13.2 us (3%)
    ppermute x7, waiting for transfers between devices, form_the_sums_all(): moved = lax.ppermute(moved, axis_name='ri', perm=m_next)  114 us
    all_gather x1, waiting for transfers between devices, body(): gathered_occ = lax.all_gather(occ_factor, ('mu', 'nu'), axis=0, tiled=True)  82.1 us
    unnamed x37, local copies, waits for them, and re-layouts  47.5 us
    unnamed x4, waiting for transfers between devices  45.6 us
    scatter-add x1, other arithmetic, slot_sum(): jax.ops.segment_sum(slab_products, segment_ids, num_segments=blocks_mu + 1)  40.7 us
    transpose x1, local copies, waits for them, and re-layouts, body(): jnp.einsum('pkab,kbo->pkao', three_center, occ_blocks, preferred_element_...  18.6 us
    dot_general x1, matrix products, body(): jnp.einsum('sm,pmo->pso', virt_kept, lax.all_gather(summed, ('mu', 'nu'),...  18.3 us
    dot_general x1, matrix products, body(): jnp.einsum('pkab,kbo->pkao', three_center, occ_blocks, preferred_element_...  13.5 us
  transfers between devices with their start and end apart: 10, of which 9 were waited for; matrix products, arithmetic and copies ran while one was open for 8% of the time, Pallas kernels for 0%

profile of v1, /device:TPU:2, one launch (start us, length us, event | category | flops | bytes accessed | tf_op | source)
XLA Modules:
  0.0 427.9 jit_solution(5961937905699308010)
XLA Ops:
  9.5 82.1 %all-gather.3.cloned.1.call-done = bf16[12288,128]{1,0:T(8,128)(2,1)} async-done(((bf16[384,128]{1,0:T(8,128)(2,1)}), bf16[12288,128]{1,0:T(8,128)(2,1)}) %all-gather.3.cloned.1.call-update) | async-done | bytes 3145744 | tf_op jit(solution)/shard_map/all_gather | solution.py:33
  91.6 8.4 %broadcast_select_fusion = bf16[12288,128]{1,0:T(8,128)(2,1)S(1)} fusion(bf16[12288,128]{1,0:T(8,128)(2,1)} %all-gather.3.cloned.1.call-done, pred[12288]{0:T(1024)(128)(4,1)S(1)} %get-tuple-element.8), kind=kLoop, calls=%fused_computation.16 | loop fusion | flops 1572864 | bytes 6303744 | tf_op jit(solution)/shard_map/jit(_where)/select_n | solution.py:34
  100.0 2.5 gather_fusion
  102.5 13.5 %fusion.10 = f32[72,4,128,128]{2,3,1,0:T(8,128)} fusion(bf16[4,72,128,128]{3,2,1,0:T(8,128)(2,1)} %param.7, bf16[72,128,128]{2,1,0:T(8,128)(2,1)} %gather_fusion), kind=kOutput, calls=%fused_computation.12 | convolution fusion | flops 1207959552 | bytes 30670848 | tf_op jit(solution)/shard_map/pkab,kbo->pkao/dot_general | solution.py:39
  116.0 18.6 %copy.19 = f32[72,4,128,128]{3,2,1,0:T(8,128)} copy(f32[72,4,128,128]{2,3,1,0:T(8,128)} %fusion.10) | data formatting | bytes 37748736 | tf_op jit(solution)/shard_map/pkab,kbo->pkao/transpose | solution.py:39
  134.7 3.5 broadcast_in_dim.21
  138.2 40.7 %scatter_fusion = f32[4,25,128,128]{3,2,1,0:T(8,128)} fusion(f32[4,25,128,128]{3,2,1,0:T(8,128)} %broadcast_in_dim.21, s32[72]{0:T(128)S(1)} %get-tuple-element.6, f32[72,4,128,128]{3,2,1,0:T(8,128)} %copy.19), kind=kCustom, calls=%fused_computation.1 | custom fusion | flops 4718592 | bytes 56623392 | tf_op jit(solution)/shard_map/vmap()/scatter-add | solution.py:46
  178.9 3.5 slice.19
  182.4 15.0 %copy.26 = bf16[4,3072,128]{2,0,1:T(4,128)(2,1)S(1)} copy(bf16[4,3072,128]{2,1,0:T(8,128)(2,1)S(1)} %bitcast.57) | data formatting | bytes 6291456
  199.9 44.9 %reduce-scatter.4.cloned.1.call-done = bf16[384,512]{1,0:T(8,128)(2,1)} async-done(((bf16[3072,512]{1,0:T(8,128)(2,1)}), bf16[384,512]{1,0:T(8,128)(2,1)}) %reduce-scatter.4.cloned.1.call-update) | async-done | bytes 393232
  246.9 16.8 %collective-permute-done = bf16[384,1536]{1,0:T(8,128)(2,1)S(1)} collective-permute-done((bf16[384,1536]{1,0:T(8,128)(2,1)S(1)}, bf16[384,1536]{1,0:T(8,128)(2,1)S(1)}, u32[]{:S(2)}, u32[]{:S(2)}) %collective-permute-start) | collective-permute-done | bytes 1179680 | tf_op jit(solution)/shard_map/ppermute | solution.py:17
  263.7 16.8 %collective-permute-done.1 = bf16[384,1536]{1,0:T(8,128)(2,1)S(1)} collective-permute-done((bf16[384,1536]{1,0:T(8,128)(2,1)S(1)}, bf16[384,1536]{1,0:T(8,128)(2,1)S(1)}, u32[]{:S(2)}, u32[]{:S(2)}) %collective-permute-start.1) | collective-permute-done | bytes 1179680 | tf_op jit(solution)/shard_map/ppermute | solution.py:17
  280.6 16.8 %collective-permute-done.2 = bf16[384,1536]{1,0:T(8,128)(2,1)S(1)} collective-permute-done((bf16[384,1536]{1,0:T(8,128)(2,1)S(1)}, bf16[384,1536]{1,0:T(8,128)(2,1)S(1)}, u32[]{:S(2)}, u32[]{:S(2)}) %collective-permute-start.2) | collective-permute-done | bytes 1179680 | tf_op jit(solution)/shard_map/ppermute | solution.py:17
  298.4 16.8 %collective-permute-done.3 = bf16[384,1536]{1,0:T(8,128)(2,1)S(1)} collective-permute-done((bf16[384,1536]{1,0:T(8,128)(2,1)S(1)}, bf16[384,1536]{1,0:T(8,128)(2,1)S(1)}, u32[]{:S(2)}, u32[]{:S(2)}) %collective-permute-start.3) | collective-permute-done | bytes 1179680 | tf_op jit(solution)/shard_map/ppermute | solution.py:17
  316.3 16.8 %collective-permute-done.4 = bf16[384,1536]{1,0:T(8,128)(2,1)S(1)} collective-permute-done((bf16[384,1536]{1,0:T(8,128)(2,1)S(1)}, bf16[384,1536]{1,0:T(8,128)(2,1)S(1)}, u32[]{:S(2)}, u32[]{:S(2)}) %collective-permute-start.4) | collective-permute-done | bytes 1179680 | tf_op jit(solution)/shard_map/ppermute | solution.py:17
  334.2 16.9 %collective-permute-done.5 = bf16[384,1536]{1,0:T(8,128)(2,1)} collective-permute-done((bf16[384,1536]{1,0:T(8,128)(2,1)S(1)}, bf16[384,1536]{1,0:T(8,128)(2,1)}, u32[]{:S(2)}, u32[]{:S(2)}) %collective-permute-start.5) | collective-permute-done | bytes 1179680 | tf_op jit(solution)/shard_map/ppermute | solution.py:17
  355.1 13.2 %collective-permute-done.6 = bf16[384,1536]{1,0:T(8,128)(2,1)} collective-permute-done((bf16[384,1536]{1,0:T(8,128)(2,1)}, bf16[384,1536]{1,0:T(8,128)(2,1)}, u32[]{:S(2)}, u32[]{:S(2)}) %collective-permute-start.6) | collective-permute-done | bytes 1179680 | tf_op jit(solution)/shard_map/ppermute | solution.py:17
  370.7 2.4 constant_dynamic-update-slice_fusion.14
  373.1 2.5 constant_dynamic-update-slice_fusion.13
  375.6 2.5 constant_dynamic-update-slice_fusion.12
  382.7 2.4 constant_dynamic-update-slice_fusion.7
  385.1 2.4 constant_dynamic-update-slice_fusion.6
  394.4 7.6 %and.66 = pred[384,96,128]{2,1,0:T(32,128)(4,1)S(1)} broadcast(pred[384,96]{1,0:T(8,128)(4,1)} %copy.21), dimensions={0,1} | broadcast | bytes 4755456 | tf_op jit(solution)/shard_map/and | solution.py:60
  402.1 18.3 %fusion.18 = bf16[4,384,128]{1,2,0:T(8,128)(2,1)S(1)} fusion(bf16[4,12288,128]{1,2,0:T(8,128)(2,1)} %all-gather.5.cloned.1.call-done, pred[48,8,96,128]{3,2,1,0:T(32,128)(4,1)S(1)} %bitcast.60, bf16[384,24576]{1,0:T(8,128)(2,1)} %constant_dynamic-update-slice_fusion, s32[]{:T(128)S(6)} %select_n.49, pred[384]{0:T(512)(128)(4,1)S(1)} %copy-done.8, ...), kind=kOutput, calls=%fused_computation.19 | convolution fusion | flops 4846190592 | bytes 27144580 | tf_op jit(solution)/shard_map/sm,pmo->pso/dot_general | solution.py:67
  (57 shorter events, 29.4 us)
Async XLA Ops:
  6.5 85.1 %all-gather.3.cloned.1.call-start = ((), (), s32[]{:S(2)}) async-start(), calls=%async_computation.1 | async-start | bytes 3244032 | tf_op jit(solution)/shard_map/all_gather | solution.py:33
  7.3 237.5 %reduce-scatter.4.cloned.1.call-start = ((), (), s32[]{:S(2)}) async-start(), calls=%async_computation.3 | async-start | bytes 3538944
  182.4 64.5 %copy-start = (bf16[384,1536]{1,0:T(8,128)(2,1)S(1)}, bf16[384,1536]{1,0:T(8,128)(2,1)}, u32[]{:S(2)}) copy-start(bf16[384,1536]{1,0:T(8,128)(2,1)} %param.10) | copy-start | bytes 3538948
  182.4 172.6 %copy-start.7 = (s32[96]{0:T(128)S(1)}, s32[96]{0:T(128)}, u32[]{:S(2)}) copy-start(s32[96]{0:T(128)} %param.11) | copy-start | bytes 1156
  199.7 194.8 %all-gather.5.cloned.1.call-start = ((), (), s32[]{:S(2)}) async-start(), calls=%async_computation.2 | async-start | bytes 12976128 | tf_op jit(solution)/shard_map/all_gather | solution.py:70
  246.9 16.9 %collective-permute-start = (bf16[384,1536]{1,0:T(8,128)(2,1)S(1)}, bf16[384,1536]{1,0:T(8,128)(2,1)S(1)}, u32[]{:S(2)}, u32[]{:S(2)}) collective-permute-start(bf16[384,1536]{1,0:T(8,128)(2,1)S(1)} %copy-done), channel_id=1, source_target_pairs={{0,32},{32,64},{64,96},{96,128},{128,160},{160,192},{192,224},{224... | collective-permute-start | bytes 3538952 | tf_op jit(solution)/shard_map/ppermute | solution.py:17
  263.7 16.8 %collective-permute-start.1 = (bf16[384,1536]{1,0:T(8,128)(2,1)S(1)}, bf16[384,1536]{1,0:T(8,128)(2,1)S(1)}, u32[]{:S(2)}, u32[]{:S(2)}) collective-permute-start(bf16[384,1536]{1,0:T(8,128)(2,1)S(1)} %collective-permute-done), channel_id=1, source_target_pairs={{0,32},{32,64},{64,96},{96,128},{128,160},{160,192},{192,224},{224... | collective-permute-start | bytes 3538952 | tf_op jit(solution)/shard_map/ppermute | solution.py:17
  280.6 16.8 %collective-permute-start.2 = (bf16[384,1536]{1,0:T(8,128)(2,1)S(1)}, bf16[384,1536]{1,0:T(8,128)(2,1)S(1)}, u32[]{:S(2)}, u32[]{:S(2)}) collective-permute-start(bf16[384,1536]{1,0:T(8,128)(2,1)S(1)} %collective-permute-done.1), channel_id=1, source_target_pairs={{0,32},{32,64},{64,96},{96,128},{128,160},{160,192},{192,224},{224... | collective-permute-start | bytes 3538952 | tf_op jit(solution)/shard_map/ppermute | solution.py:17
  297.4 1.0 copy-start.1
  298.4 16.8 %collective-permute-start.3 = (bf16[384,1536]{1,0:T(8,128)(2,1)S(1)}, bf16[384,1536]{1,0:T(8,128)(2,1)S(1)}, u32[]{:S(2)}, u32[]{:S(2)}) collective-permute-start(bf16[384,1536]{1,0:T(8,128)(2,1)S(1)} %collective-permute-done.2), channel_id=1, source_target_pairs={{0,32},{32,64},{64,96},{96,128},{128,160},{160,192},{192,224},{224... | collective-permute-start | bytes 3538952 | tf_op jit(solution)/shard_map/ppermute | solution.py:17
  315.3 1.0 copy-start.3
  316.3 16.8 %collective-permute-start.4 = (bf16[384,1536]{1,0:T(8,128)(2,1)S(1)}, bf16[384,1536]{1,0:T(8,128)(2,1)S(1)}, u32[]{:S(2)}, u32[]{:S(2)}) collective-permute-start(bf16[384,1536]{1,0:T(8,128)(2,1)S(1)} %collective-permute-done.3), channel_id=1, source_target_pairs={{0,32},{32,64},{64,96},{96,128},{128,160},{160,192},{192,224},{224... | collective-permute-start | bytes 3538952 | tf_op jit(solution)/shard_map/ppermute | solution.py:17
  333.2 1.1 copy-start.5
  334.2 16.9 %collective-permute-start.5 = (bf16[384,1536]{1,0:T(8,128)(2,1)S(1)}, bf16[384,1536]{1,0:T(8,128)(2,1)}, u32[]{:S(2)}, u32[]{:S(2)}) collective-permute-start(bf16[384,1536]{1,0:T(8,128)(2,1)S(1)} %collective-permute-done.4), channel_id=1, source_target_pairs={{0,32},{32,64},{64,96},{96,128},{128,160},{160,192},{192,224},{224... | collective-permute-start | bytes 3538952 | tf_op jit(solution)/shard_map/ppermute | solution.py:17
  351.2 17.2 %collective-permute-start.6 = (bf16[384,1536]{1,0:T(8,128)(2,1)}, bf16[384,1536]{1,0:T(8,128)(2,1)}, u32[]{:S(2)}, u32[]{:S(2)}) collective-permute-start(bf16[384,1536]{1,0:T(8,128)(2,1)} %collective-permute-done.5), channel_id=1, source_target_pairs={{0,32},{32,64},{64,96},{96,128},{128,160},{160,192},{192,224},{224... | collective-permute-start | bytes 3538952 | tf_op jit(solution)/shard_map/ppermute | solution.py:17
  354.4 23.7 %copy-start.2 = (bf16[384,1536]{1,0:T(8,128)(2,1)S(1)}, bf16[384,1536]{1,0:T(8,128)(2,1)}, u32[]{:S(2)}) copy-start(bf16[384,1536]{1,0:T(8,128)(2,1)} %copy-done.1) | copy-start | bytes 3538948
  373.1 14.4 %copy-start.6 = (bf16[384,1536]{1,0:T(8,128)(2,1)S(1)}, bf16[384,1536]{1,0:T(8,128)(2,1)}, u32[]{:S(2)}) copy-start(bf16[384,1536]{1,0:T(8,128)(2,1)} %copy-done.5) | copy-start | bytes 3538948
  375.6 13.1 %copy-start.4 = (bf16[384,1536]{1,0:T(8,128)(2,1)S(1)}, bf16[384,1536]{1,0:T(8,128)(2,1)}, u32[]{:S(2)}) copy-start(bf16[384,1536]{1,0:T(8,128)(2,1)} %copy-done.3) | copy-start | bytes 3538948
  387.5 14.5 %copy-start.8 = (pred[384]{0:T(512)(128)(4,1)S(1)}, pred[384]{0:T(512)(128)(4,1)}, u32[]{:S(2)}) copy-start(pred[384]{0:T(512)(128)(4,1)} %dynamic_slice.7) | copy-start | bytes 1156
Sparse Core Ops, SparseCore 0:
  9.9 81.6 all-gather.2
  199.8 44.9 reduce-scatter.3
  247.3 124.6 all-gather.4
